TPU v7x, 32 devices: a whole 2x2x4 slice. The times are simulated.
32 devices in a mesh: segment: 4 (over x, core), strip: 8 (over z, y).
Axes of the slice: x: 2, y: 2, z: 4, core: 2. Of those that a mesh axis runs over, the one named last changes fastest.
Arguments:
- features: bfloat16 [2, 256, 128, 256], P(None, 'segment', 'strip'), may hold values from -6 to 6
- weight_first: bfloat16 [3, 3, 256, 256], replicated, may hold values from -0.125 to 0.125
- weight_second: bfloat16 [3, 3, 256, 256], replicated, may hold values from -0.125 to 0.125
- weight_down: bfloat16 [2, 2, 256, 512], replicated, may hold values from -0.1875 to 0.1875
- section_weights: bfloat16 [4, 3, 3, 512, 512], P('segment'), may hold values from -0.09375 to 0.09375
Outputs:
- section_features: bfloat16 [4, 2, 128, 64, 512], P('segment', None, 'strip')
All inputs are finite; a program needn't handle non-finite values.
Results may differ from a plain program's by a relative error of at most 0.0095.
Values may be sent and summed in bfloat16 or wider, within the bound.
A program may use at most 128 MiB of HBM per device.

v0:
```python
import jax
import jax.numpy as jnp
from jax import lax
from jax.sharding import PartitionSpec as P


def padded_2(block, sides, width):
    for axis, dim in sides:
        count = lax.axis_size(axis)
        forward = [(i, i + 1) for i in range(count - 1)]
        backward = [(target, source) for source, target in forward]
        low = lax.ppermute(
            lax.slice_in_dim(block, block.shape[dim] - width, None, axis=dim), axis, forward
        )
        high = lax.ppermute(lax.slice_in_dim(block, 0, width, axis=dim), axis, backward)
        block = jnp.concatenate([low, block, high], axis=dim)
    return block


def passed_along(value, axis, steps):
    count = lax.axis_size(axis)
    first, last = (max(0, -steps), min(count, count - steps))
    return lax.ppermute(value, axis, [(source, source + steps) for source in range(first, last)])


def conv_valid(padded, weight):
    batches, rows_pad, columns_pad, channels = padded.shape
    rows = rows_pad - 2
    columns = columns_pad - 2
    total = None
    for row_off in range(3):
        for col_off in range(3):
            window = padded[:, row_off : row_off + rows, col_off : col_off + columns, :].reshape(
                -1, channels
            )
            partial_sum = jnp.dot(
                window, weight[row_off, col_off], preferred_element_type=jnp.float32
            )
            total = partial_sum if total is None else total + partial_sum
    return total.reshape(batches, rows, columns, weight.shape[3])


def residual_valid(padded, inner, weight):
    return jax.nn.relu(inner.astype(jnp.float32) + conv_valid(padded, weight))


def tile_rimmed(inputs):
    return padded_2(inputs, (("segment", 1), ("strip", 2)), 1)


def section_layer(current, weight):
    rimmed = padded_2(current, (("strip", 0),), 1)
    padded = jnp.pad(rimmed, ((0, 0), (1, 1), (0, 0)))
    return residual_valid(padded[None], current[None], weight)[0]


def shards(features, weight_first, weight_second, weight_down, section_weights):
    batches, tile_rows, tile_columns, channels = features.shape
    first = residual_valid(tile_rimmed(features), features, weight_first).astype(jnp.bfloat16)
    second = residual_valid(tile_rimmed(first), first, weight_second).astype(jnp.bfloat16)
    blocks = second.reshape(batches, tile_rows // 2, 2, tile_columns // 2, 2, channels)
    total = None
    for row_off in range(2):
        for col_off in range(2):
            piece = blocks[:, :, row_off, :, col_off, :].reshape(-1, channels)
            partial_sum = jnp.dot(
                piece, weight_down[row_off, col_off], preferred_element_type=jnp.float32
            )
            total = partial_sum if total is None else total + partial_sum
    out_channels = weight_down.shape[3]
    reduced = (
        jax.nn.relu(total)
        .reshape(batches, tile_rows // 2, tile_columns // 2, out_channels)
        .astype(jnp.bfloat16)
    )
    banded = lax.all_gather(reduced, "segment", axis=1, tiled=True)
    strips = lax.all_to_all(banded, "strip", split_axis=1, concat_axis=2, tiled=True)
    strip_rows = strips.shape[1]
    full_columns = strips.shape[2]
    weight = section_weights[0]
    segment_index = lax.axis_index("segment")
    segments = lax.axis_size("segment")
    results = jnp.zeros((batches, strip_rows, full_columns, out_channels), jnp.bfloat16)
    inputs = [strips[window_index] for window_index in range(batches)]
    micro_count = len(inputs)
    ticks = micro_count + segments - 1
    carried = jnp.zeros_like(inputs[0])
    zero_index = jnp.int32(0)
    for instant in range(ticks):
        feed = inputs[min(instant, micro_count - 1)]
        current = jnp.where(segment_index == 0, feed, carried)
        produced = section_layer(current, weight)
        micro_index = instant - segment_index
        valid = (micro_index >= 0) & (micro_index < micro_count)
        slot = jnp.clip(micro_index, 0, micro_count - 1)
        produced = produced.astype(jnp.bfloat16)
        anchor = (slot, zero_index, zero_index, zero_index)
        previous = lax.dynamic_slice(results, anchor, (1, strip_rows, full_columns, out_channels))
        chosen = jnp.where(valid, produced[None], previous)
        results = lax.dynamic_update_slice(results, chosen, anchor)
        if instant < ticks - 1:
            carried = passed_along(produced, "segment", 1)
    return results[None]


def solution(mesh):
    return jax.shard_map(
        shards,
        mesh=mesh,
        in_specs=(
            P(None, "segment", "strip", None),
            P(),
            P(),
            P(),
            P("segment", None, None, None, None),
        ),
        out_specs=P("segment", None, "strip", None, None),
        check_vma=False,
    )
```

profile of v0, /device:TPU:6, one launch (start us, length us, event | category | flops | bytes accessed | tf_op | source)
XLA Modules:
  0.0 333.1 jit_solution(16539917198807807263)
XLA Ops:
  7.3 1.9 collective-permute-start
  9.2 3.6 %collective-permute-start.1 = (bf16[2,1,16,256]{3,2,1,0:T(8,128)(2,1)S(1)}, bf16[2,1,16,256]{3,2,1,0:T(8,128)(2,1)S(1)}, u32[]{:S(2)}, u32[]{:S(2)}) collective-permute-start(bf16[2,1,16,256]{3,2,1,0:T(8,128)(2,1)S(1)} %get-tuple-element.101), channel_id=1, source_target_pairs={{8,0},{16,8},{24,16},{9,1},{17,9},{25,17},{10,2},{18,10},{26,18},{... | collective-permute-start | bytes 49160 | tf_op jit(solution)/shard_map/ppermute | solution.py:15
  14.3 2.2 pad_maximum_fusion.4
  16.8 3.4 %collective-permute-start.2 = (bf16[2,66,1,256]{3,1,2,0:T(8,128)(2,1)S(1)}, bf16[2,66,1,256]{3,1,2,0:T(8,128)(2,1)S(1)}, u32[]{:S(2)}, u32[]{:S(2)}) collective-permute-start(bf16[2,66,1,256]{3,1,2,0:T(8,128)(2,1)S(1)} %copy.48), channel_id=1, source_target_pairs={{0,1},{1,2},{2,3},{3,4},{4,5},{5,6},{6,7},{8,9},{9,10},{10,11},{11... | collective-permute-start | bytes 202760 | tf_op jit(solution)/shard_map/ppermute | solution.py:12
  20.2 2.4 collective-permute-start.3
  23.1 4.2 %collective-permute-done.3 = bf16[2,66,1,256]{3,1,2,0:T(8,128)(2,1)S(1)} collective-permute-done((bf16[2,66,1,256]{3,1,2,0:T(8,128)(2,1)S(1)}, bf16[2,66,1,256]{3,1,2,0:T(8,128)(2,1)S(1)}, u32[]{:S(2)}, u32[]{:S(2)}) %collective-permute-start.3) | collective-permute-done | bytes 67616 | tf_op jit(solution)/shard_map/ppermute | solution.py:15
  27.5 3.3 %pad_maximum_fusion.5 = (bf16[2,64,16,256]{3,2,1,0:T(8,128)(2,1)S(1)}, bf16[2,64,16,256]{3,2,1,0:T(8,128)(2,1)S(1)}, bf16[2,64,16,256]{3,2,1,0:T(8,128)(2,1)S(1)...) fusion(bf16[2,66,16,256]{3,2,1,0:T(8,128)(2,1)S(1)} %constant_d, ...), kind=kLoop, calls=%fused_computation.79 | loop fusion | flops 12582912 | bytes 7507968 | tf_op jit(solution)/shard_map/concatenate | solution.py:16
  36.2 1.9 collective-permute-start.4
  38.1 3.6 %collective-permute-start.5 = (bf16[2,1,16,256]{3,2,1,0:T(8,128)(2,1)S(1)}, bf16[2,1,16,256]{3,2,1,0:T(8,128)(2,1)S(1)}, u32[]{:S(2)}, u32[]{:S(2)}) collective-permute-start(bf16[2,1,16,256]{3,2,1,0:T(8,128)(2,1)S(1)} %get-tuple-element.97), channel_id=1, source_target_pairs={{8,0},{16,8},{24,16},{9,1},{17,9},{25,17},{10,2},{18,10},{26,18},{... | collective-permute-start | bytes 49160 | tf_op jit(solution)/shard_map/ppermute | solution.py:15
  43.4 2.5 collective-permute-start.6
  46.0 3.5 %collective-permute-start.7 = (bf16[2,66,1,256]{3,1,2,0:T(8,128)(2,1)S(1)}, bf16[2,66,1,256]{3,1,2,0:T(8,128)(2,1)S(1)}, u32[]{:S(2)}, u32[]{:S(2)}) collective-permute-start(bf16[2,66,1,256]{3,1,2,0:T(8,128)(2,1)S(1)} %copy.54), channel_id=1, source_target_pairs={{1,0},{2,1},{3,2},{4,3},{5,4},{6,5},{7,6},{9,8},{10,9},{11,10},{12... | collective-permute-start | bytes 202760 | tf_op jit(solution)/shard_map/ppermute | solution.py:15
  50.5 2.6 collective-permute-done.7
  64.5 22.0 %all-gather.2.cloned.1.call-done = bf16[2,128,8,512]{3,2,0,1:T(8,128)(2,1)} async-done(((bf16[2,32,8,512]{3,2,0,1:T(8,128)(2,1)}), bf16[2,128,8,512]{3,2,0,1:T(8,128)(2,1)}) %all-gather.2.cloned.1.call-update) | async-done | bytes 2097168 | tf_op jit(solution)/shard_map/all_gather | solution.py:76
  86.5 6.1 %all-to-all-start = ((bf16[2,128,8,512]{3,2,0,1:T(8,128)(2,1)}), bf16[2,128,8,512]{3,2,0,1:T(8,128)(2,1)S(1)}, u32[]{:S(2)}, u32[]{:S(2)}) async-start(bf16[2,128,8,512]{3,2,0,1:T(8,128)(2,1)} %all-gather.2.cloned.1.call-done), calls=%async_computation | async-start | bytes 4194304 | tf_op jit(solution)/shard_map/all_to_all | solution.py:77
  92.6 48.1 %all-to-all-done = bf16[2,128,8,512]{3,2,0,1:T(8,128)(2,1)S(1)} async-done(((bf16[2,128,8,512]{3,2,0,1:T(8,128)(2,1)}), bf16[2,128,8,512]{3,2,0,1:T(8,128)(2,1)S(1)}, u32[]{:S(2)}, u32[]{:S(2)}) %all-to-all-start) | async-done | bytes 2097184 | tf_op jit(solution)/shard_map/all_to_all | solution.py:77
  142.3 1.9 collective-permute-start.8
  144.2 4.1 %collective-permute-start.9 = (bf16[1,64,512]{2,1,0:T(8,128)(2,1)S(1)}, bf16[1,64,512]{2,1,0:T(8,128)(2,1)S(1)}, u32[]{:S(2)}, u32[]{:S(2)}) collective-permute-start(bf16[1,64,512]{2,1,0:T(8,128)(2,1)S(1)} %get-tuple-element.89), channel_id=1, source_target_pairs={{1,0},{2,1},{3,2},{4,3},{5,4},{6,5},{7,6},{9,8},{10,9},{11,10},{12... | collective-permute-start | bytes 196616 | tf_op jit(solution)/shard_map/ppermute | solution.py:15
  148.5 2.8 collective-permute-done.9
  151.8 2.4 fusion.121
  162.8 1.9 collective-permute-start.10
  164.7 14.5 %collective-permute-done.10 = bf16[16,64,512]{2,1,0:T(8,128)(2,1)} collective-permute-done((bf16[16,64,512]{2,1,0:T(8,128)(2,1)}, bf16[16,64,512]{2,1,0:T(8,128)(2,1)}, u32[]{:S(2)}, u32[]{:S(2)}) %collective-permute-start.10) | collective-permute-done | bytes 1048608 | tf_op jit(solution)/shard_map/ppermute | solution.py:23
  180.7 2.1 collective-permute-start.11
  182.8 4.2 %collective-permute-start.12 = (bf16[1,64,512]{2,1,0:T(8,128)(2,1)S(1)}, bf16[1,64,512]{2,1,0:T(8,128)(2,1)S(1)}, u32[]{:S(2)}, u32[]{:S(2)}) collective-permute-start(bf16[1,64,512]{2,1,0:T(8,128)(2,1)S(1)} %get-tuple-element.87), channel_id=1, source_target_pairs={{1,0},{2,1},{3,2},{4,3},{5,4},{6,5},{7,6},{9,8},{10,9},{11,10},{12... | collective-permute-start | bytes 196616 | tf_op jit(solution)/shard_map/ppermute | solution.py:15
  187.8 2.0 collective-permute-done.12
  190.4 2.4 fusion.120
  200.4 1.9 collective-permute-start.13
  202.3 14.2 %collective-permute-done.13 = bf16[16,64,512]{2,1,0:T(8,128)(2,1)S(1)} collective-permute-done((bf16[16,64,512]{2,1,0:T(8,128)(2,1)S(1)}, bf16[16,64,512]{2,1,0:T(8,128)(2,1)S(1)}, u32[]{:S(2)}, u32[]{:S(2)}) %collective-permute-start.13) | collective-permute-done | bytes 1048608 | tf_op jit(solution)/shard_map/ppermute | solution.py:23
  218.5 2.7 collective-permute-start.14
  221.2 3.5 %collective-permute-start.15 = (bf16[1,64,512]{2,1,0:T(8,128)(2,1)S(1)}, bf16[1,64,512]{2,1,0:T(8,128)(2,1)S(1)}, u32[]{:S(2)}, u32[]{:S(2)}) collective-permute-start(bf16[1,64,512]{2,1,0:T(8,128)(2,1)S(1)} %get-tuple-element.85), channel_id=1, source_target_pairs={{1,0},{2,1},{3,2},{4,3},{5,4},{6,5},{7,6},{9,8},{10,9},{11,10},{12... | collective-permute-start | bytes 196616 | tf_op jit(solution)/shard_map/ppermute | solution.py:15
  224.7 3.6 %collective-permute-done.15 = bf16[1,64,512]{2,1,0:T(8,128)(2,1)S(1)} collective-permute-done((bf16[1,64,512]{2,1,0:T(8,128)(2,1)S(1)}, bf16[1,64,512]{2,1,0:T(8,128)(2,1)S(1)}, u32[]{:S(2)}, u32[]{:S(2)}) %collective-permute-start.15) | collective-permute-done | bytes 65568 | tf_op jit(solution)/shard_map/ppermute | solution.py:15
  228.2 1.7 fusion.8
  230.0 2.4 fusion.119
  239.2 2.0 fusion.23
  241.3 1.9 collective-permute-start.16
  243.2 14.2 %collective-permute-done.16 = bf16[16,64,512]{2,1,0:T(8,128)(2,1)S(1)} collective-permute-done((bf16[16,64,512]{2,1,0:T(8,128)(2,1)S(1)}, bf16[16,64,512]{2,1,0:T(8,128)(2,1)S(1)}, u32[]{:S(2)}, u32[]{:S(2)}) %collective-permute-start.16) | collective-permute-done | bytes 1048608 | tf_op jit(solution)/shard_map/ppermute | solution.py:23
  259.4 3.6 %collective-permute-start.17 = (bf16[1,64,512]{2,1,0:T(8,128)(2,1)S(1)}, bf16[1,64,512]{2,1,0:T(8,128)(2,1)S(1)}, u32[]{:S(2)}, u32[]{:S(2)}) collective-permute-start(bf16[1,64,512]{2,1,0:T(8,128)(2,1)S(1)} %get-tuple-element.82), channel_id=1, source_target_pairs={{0,1},{1,2},{2,3},{3,4},{4,5},{5,6},{6,7},{8,9},{9,10},{10,11},{11... | collective-permute-start | bytes 196616 | tf_op jit(solution)/shard_map/ppermute | solution.py:12
  263.1 2.7 collective-permute-start.18
  265.8 4.3 %collective-permute-done.18 = bf16[1,64,512]{2,1,0:T(8,128)(2,1)S(1)} collective-permute-done((bf16[1,64,512]{2,1,0:T(8,128)(2,1)S(1)}, bf16[1,64,512]{2,1,0:T(8,128)(2,1)S(1)}, u32[]{:S(2)}, u32[]{:S(2)}) %collective-permute-start.18) | collective-permute-done | bytes 65568 | tf_op jit(solution)/shard_map/ppermute | solution.py:15
  270.1 1.7 fusion.7
  271.8 2.4 fusion.118
  281.1 2.0 fusion.22
  283.1 1.9 collective-permute-start.19
  285.1 14.2 %collective-permute-done.19 = bf16[16,64,512]{2,1,0:T(8,128)(2,1)S(1)} collective-permute-done((bf16[16,64,512]{2,1,0:T(8,128)(2,1)S(1)}, bf16[16,64,512]{2,1,0:T(8,128)(2,1)S(1)}, u32[]{:S(2)}, u32[]{:S(2)}) %collective-permute-start.19) | collective-permute-done | bytes 1048608 | tf_op jit(solution)/shard_map/ppermute | solution.py:23
  301.3 3.9 %collective-permute-start.20 = (bf16[1,64,512]{2,1,0:T(8,128)(2,1)S(1)}, bf16[1,64,512]{2,1,0:T(8,128)(2,1)S(1)}, u32[]{:S(2)}, u32[]{:S(2)}) collective-permute-start(bf16[1,64,512]{2,1,0:T(8,128)(2,1)S(1)} %get-tuple-element.80), channel_id=1, source_target_pairs={{0,1},{1,2},{2,3},{3,4},{4,5},{5,6},{6,7},{8,9},{9,10},{10,11},{11... | collective-permute-start | bytes 196616 | tf_op jit(solution)/shard_map/ppermute | solution.py:12
  305.2 2.1 collective-permute-start.21
  308.7 3.6 %collective-permute-done.21 = bf16[1,64,512]{2,1,0:T(8,128)(2,1)S(1)} collective-permute-done((bf16[1,64,512]{2,1,0:T(8,128)(2,1)S(1)}, bf16[1,64,512]{2,1,0:T(8,128)(2,1)S(1)}, u32[]{:S(2)}, u32[]{:S(2)}) %collective-permute-start.21) | collective-permute-done | bytes 65568 | tf_op jit(solution)/shard_map/ppermute | solution.py:15
  314.0 2.4 fusion.117
  323.3 2.8 fusion.19
  (172 shorter events, 72.9 us)
Async XLA Ops:
  6.5 80.0 %all-gather.2.cloned.1.call-start = ((), (), s32[]{:S(2)}) async-start(), calls=%async_computation.1 | async-start | bytes 2621440 | tf_op jit(solution)/shard_map/all_gather | solution.py:76
  7.3 5.6 %collective-permute-start = (bf16[2,1,16,256]{3,2,1,0:T(8,128)(2,1)S(1)}, bf16[2,1,16,256]{3,2,1,0:T(8,128)(2,1)S(1)}, u32[]{:S(2)}, u32[]{:S(2)}) collective-permute-start(bf16[2,1,16,256]{3,2,1,0:T(8,128)(2,1)S(1)} %get-tuple-element.102), channel_id=1, source_target_pairs={{0,8},{8,16},{16,24},{1,9},{9,17},{17,25},{2,10},{10,18},{18,26},{... | collective-permute-start | bytes 49160 | tf_op jit(solution)/shard_map/ppermute | solution.py:12
  9.2 5.1 %collective-permute-start.1 = (bf16[2,1,16,256]{3,2,1,0:T(8,128)(2,1)S(1)}, bf16[2,1,16,256]{3,2,1,0:T(8,128)(2,1)S(1)}, u32[]{:S(2)}, u32[]{:S(2)}) collective-permute-start(bf16[2,1,16,256]{3,2,1,0:T(8,128)(2,1)S(1)} %get-tuple-element.101), channel_id=1, source_target_pairs={{8,0},{16,8},{24,16},{9,1},{17,9},{25,17},{10,2},{18,10},{26,18},{... | collective-permute-start | bytes 49160 | tf_op jit(solution)/shard_map/ppermute | solution.py:15
  16.8 6.2 %collective-permute-start.2 = (bf16[2,66,1,256]{3,1,2,0:T(8,128)(2,1)S(1)}, bf16[2,66,1,256]{3,1,2,0:T(8,128)(2,1)S(1)}, u32[]{:S(2)}, u32[]{:S(2)}) collective-permute-start(bf16[2,66,1,256]{3,1,2,0:T(8,128)(2,1)S(1)} %copy.48), channel_id=1, source_target_pairs={{0,1},{1,2},{2,3},{3,4},{4,5},{5,6},{6,7},{8,9},{9,10},{10,11},{11... | collective-permute-start | bytes 202760 | tf_op jit(solution)/shard_map/ppermute | solution.py:12
  20.2 7.1 %collective-permute-start.3 = (bf16[2,66,1,256]{3,1,2,0:T(8,128)(2,1)S(1)}, bf16[2,66,1,256]{3,1,2,0:T(8,128)(2,1)S(1)}, u32[]{:S(2)}, u32[]{:S(2)}) collective-permute-start(bf16[2,66,1,256]{3,1,2,0:T(8,128)(2,1)S(1)} %copy.50), channel_id=1, source_target_pairs={{1,0},{2,1},{3,2},{4,3},{5,4},{6,5},{7,6},{9,8},{10,9},{11,10},{12... | collective-permute-start | bytes 202760 | tf_op jit(solution)/shard_map/ppermute | solution.py:15
  27.5 3.4 %copy-start.8 = (bf16[3,3,256,256]{3,2,1,0:T(8,128)(2,1)S(1)}, bf16[3,3,256,256]{3,2,1,0:T(8,128)(2,1)}, u32[]{:S(2)}) copy-start(bf16[3,3,256,256]{3,2,1,0:T(8,128)(2,1)} %param.6) | copy-start | bytes 3538948
  32.6 1.2 copy-start.6
  36.2 5.6 %collective-permute-start.4 = (bf16[2,1,16,256]{3,2,1,0:T(8,128)(2,1)S(1)}, bf16[2,1,16,256]{3,2,1,0:T(8,128)(2,1)S(1)}, u32[]{:S(2)}, u32[]{:S(2)}) collective-permute-start(bf16[2,1,16,256]{3,2,1,0:T(8,128)(2,1)S(1)} %get-tuple-element.96), channel_id=1, source_target_pairs={{0,8},{8,16},{16,24},{1,9},{9,17},{17,25},{2,10},{10,18},{18,26},{... | collective-permute-start | bytes 49160 | tf_op jit(solution)/shard_map/ppermute | solution.py:12
  38.1 5.1 %collective-permute-start.5 = (bf16[2,1,16,256]{3,2,1,0:T(8,128)(2,1)S(1)}, bf16[2,1,16,256]{3,2,1,0:T(8,128)(2,1)S(1)}, u32[]{:S(2)}, u32[]{:S(2)}) collective-permute-start(bf16[2,1,16,256]{3,2,1,0:T(8,128)(2,1)S(1)} %get-tuple-element.97), channel_id=1, source_target_pairs={{8,0},{16,8},{24,16},{9,1},{17,9},{25,17},{10,2},{18,10},{26,18},{... | collective-permute-start | bytes 49160 | tf_op jit(solution)/shard_map/ppermute | solution.py:15
  43.4 7.0 %collective-permute-start.6 = (bf16[2,66,1,256]{3,1,2,0:T(8,128)(2,1)S(1)}, bf16[2,66,1,256]{3,1,2,0:T(8,128)(2,1)S(1)}, u32[]{:S(2)}, u32[]{:S(2)}) collective-permute-start(bf16[2,66,1,256]{3,1,2,0:T(8,128)(2,1)S(1)} %copy.52), channel_id=1, source_target_pairs={{0,1},{1,2},{2,3},{3,4},{4,5},{5,6},{6,7},{8,9},{9,10},{10,11},{11... | collective-permute-start | bytes 202760 | tf_op jit(solution)/shard_map/ppermute | solution.py:12
  46.0 7.1 %collective-permute-start.7 = (bf16[2,66,1,256]{3,1,2,0:T(8,128)(2,1)S(1)}, bf16[2,66,1,256]{3,1,2,0:T(8,128)(2,1)S(1)}, u32[]{:S(2)}, u32[]{:S(2)}) collective-permute-start(bf16[2,66,1,256]{3,1,2,0:T(8,128)(2,1)S(1)} %copy.54), channel_id=1, source_target_pairs={{1,0},{2,1},{3,2},{4,3},{5,4},{6,5},{7,6},{9,8},{10,9},{11,10},{12... | collective-permute-start | bytes 202760 | tf_op jit(solution)/shard_map/ppermute | solution.py:15
  54.3 1.3 copy-start.9
  61.2 1.2 copy-start.10
  86.5 54.1 %all-to-all-start = ((bf16[2,128,8,512]{3,2,0,1:T(8,128)(2,1)}), bf16[2,128,8,512]{3,2,0,1:T(8,128)(2,1)S(1)}, u32[]{:S(2)}, u32[]{:S(2)}) async-start(bf16[2,128,8,512]{3,2,0,1:T(8,128)(2,1)} %all-gather.2.cloned.1.call-done), calls=%async_computation | async-start | bytes 4194304 | tf_op jit(solution)/shard_map/all_to_all | solution.py:77
  142.3 37.0 %copy-start = (bf16[1,16,8,8,512]{4,3,0,1,2:T(8,128)(2,1)}, bf16[1,16,8,8,512]{4,3,0,1,2:T(8,128)(2,1)S(1)}, u32[]{:S(2)}) copy-start(bf16[1,16,8,8,512]{4,3,0,1,2:T(8,128)(2,1)S(1)} %get-tuple-element.13) | copy-start | bytes 3145732
  142.3 6.2 %collective-permute-start.8 = (bf16[1,64,512]{2,1,0:T(8,128)(2,1)S(1)}, bf16[1,64,512]{2,1,0:T(8,128)(2,1)S(1)}, u32[]{:S(2)}, u32[]{:S(2)}) collective-permute-start(bf16[1,64,512]{2,1,0:T(8,128)(2,1)S(1)} %get-tuple-element.88), channel_id=1, source_target_pairs={{0,1},{1,2},{2,3},{3,4},{4,5},{5,6},{6,7},{8,9},{9,10},{10,11},{11... | collective-permute-start | bytes 196616 | tf_op jit(solution)/shard_map/ppermute | solution.py:12
  144.2 7.1 %collective-permute-start.9 = (bf16[1,64,512]{2,1,0:T(8,128)(2,1)S(1)}, bf16[1,64,512]{2,1,0:T(8,128)(2,1)S(1)}, u32[]{:S(2)}, u32[]{:S(2)}) collective-permute-start(bf16[1,64,512]{2,1,0:T(8,128)(2,1)S(1)} %get-tuple-element.89), channel_id=1, source_target_pairs={{1,0},{2,1},{3,2},{4,3},{5,4},{6,5},{7,6},{9,8},{10,9},{11,10},{12... | collective-permute-start | bytes 196616 | tf_op jit(solution)/shard_map/ppermute | solution.py:15
  151.3 3.0 slice-start
  151.8 2.4 slice-start.1
  161.1 1.7 copy-start.4
  162.8 16.4 %collective-permute-start.10 = (bf16[16,64,512]{2,1,0:T(8,128)(2,1)}, bf16[16,64,512]{2,1,0:T(8,128)(2,1)}, u32[]{:S(2)}, u32[]{:S(2)}) collective-permute-start(bf16[16,64,512]{2,1,0:T(8,128)(2,1)} %maximum_convert_fusion.4), channel_id=1, source_target_pairs={{0,8},{8,16},{16,24},{1,9},{9,17},{17,25},{2,10},{10,18},{18,26},{... | collective-permute-start | bytes 3145736 | tf_op jit(solution)/shard_map/ppermute | solution.py:23
  179.2 8.0 %copy-start.5 = (f32[1024,512]{1,0:T(8,128)S(1)}, f32[1024,512]{1,0:T(8,128)}, u32[]{:S(2)}) copy-start(f32[1024,512]{1,0:T(8,128)} %copy-done.4) | copy-start | bytes 6291460
  179.2 8.0 %copy-start.7 = (f32[1,16,8,8,512]{4,3,0,1,2:T(8,128)S(1)}, f32[1,16,8,8,512]{4,3,0,1,2:T(8,128)}, u32[]{:S(2)}) copy-start(f32[1,16,8,8,512]{4,3,0,1,2:T(8,128)} %get-tuple-element.11) | copy-start | bytes 6291460
  180.7 7.1 %collective-permute-start.11 = (bf16[1,64,512]{2,1,0:T(8,128)(2,1)S(1)}, bf16[1,64,512]{2,1,0:T(8,128)(2,1)S(1)}, u32[]{:S(2)}, u32[]{:S(2)}) collective-permute-start(bf16[1,64,512]{2,1,0:T(8,128)(2,1)S(1)} %get-tuple-element.86), channel_id=1, source_target_pairs={{0,1},{1,2},{2,3},{3,4},{4,5},{5,6},{6,7},{8,9},{9,10},{10,11},{11... | collective-permute-start | bytes 196616 | tf_op jit(solution)/shard_map/ppermute | solution.py:12
  182.8 7.1 %collective-permute-start.12 = (bf16[1,64,512]{2,1,0:T(8,128)(2,1)S(1)}, bf16[1,64,512]{2,1,0:T(8,128)(2,1)S(1)}, u32[]{:S(2)}, u32[]{:S(2)}) collective-permute-start(bf16[1,64,512]{2,1,0:T(8,128)(2,1)S(1)} %get-tuple-element.87), channel_id=1, source_target_pairs={{1,0},{2,1},{3,2},{4,3},{5,4},{6,5},{7,6},{9,8},{10,9},{11,10},{12... | collective-permute-start | bytes 196616 | tf_op jit(solution)/shard_map/ppermute | solution.py:15
  187.2 5.6 %slice-start.2 = ((s8[4718592]{0:T(1024)(128)(4,1)}), s8[4194304]{0:T(1024)(128)(4,1)S(1)}, s32[]{:S(2)}) async-start(s8[4718592]{0:T(1024)(128)(4,1)} %bitcast.347), calls=%async_computation.4 | async-start | bytes 8388608
  190.4 2.4 slice-start.3
  199.7 16.8 %copy-start.1 = (bf16[1,16,8,8,512]{4,3,0,1,2:T(8,128)(2,1)S(1)}, bf16[1,16,8,8,512]{4,3,0,1,2:T(8,128)(2,1)}, u32[]{:S(2)}) copy-start(bf16[1,16,8,8,512]{4,3,0,1,2:T(8,128)(2,1)} %copy-done) | copy-start | bytes 3145732
  200.4 16.1 %collective-permute-start.13 = (bf16[16,64,512]{2,1,0:T(8,128)(2,1)S(1)}, bf16[16,64,512]{2,1,0:T(8,128)(2,1)S(1)}, u32[]{:S(2)}, u32[]{:S(2)}) collective-permute-start(bf16[16,64,512]{2,1,0:T(8,128)(2,1)S(1)} %get-tuple-element.10), channel_id=1, source_target_pairs={{0,8},{8,16},{16,24},{1,9},{9,17},{17,25},{2,10},{10,18},{18,26},{... | collective-permute-start | bytes 3145736 | tf_op jit(solution)/shard_map/ppermute | solution.py:23
  216.5 15.9 %slice-start.4 = ((s8[4718592]{0:T(1024)(128)(4,1)}), s8[524288]{0:T(1024)(128)(4,1)S(1)}, s32[]{:S(2)}) async-start(s8[4718592]{0:T(1024)(128)(4,1)} %bitcast.358), calls=%async_computation.6 | async-start | bytes 1048576
  218.5 6.2 %collective-permute-start.14 = (bf16[1,64,512]{2,1,0:T(8,128)(2,1)S(1)}, bf16[1,64,512]{2,1,0:T(8,128)(2,1)S(1)}, u32[]{:S(2)}, u32[]{:S(2)}) collective-permute-start(bf16[1,64,512]{2,1,0:T(8,128)(2,1)S(1)} %get-tuple-element.84), channel_id=1, source_target_pairs={{0,1},{1,2},{2,3},{3,4},{4,5},{5,6},{6,7},{8,9},{9,10},{10,11},{11... | collective-permute-start | bytes 196616 | tf_op jit(solution)/shard_map/ppermute | solution.py:12
  221.2 7.1 %collective-permute-start.15 = (bf16[1,64,512]{2,1,0:T(8,128)(2,1)S(1)}, bf16[1,64,512]{2,1,0:T(8,128)(2,1)S(1)}, u32[]{:S(2)}, u32[]{:S(2)}) collective-permute-start(bf16[1,64,512]{2,1,0:T(8,128)(2,1)S(1)} %get-tuple-element.85), channel_id=1, source_target_pairs={{1,0},{2,1},{3,2},{4,3},{5,4},{6,5},{7,6},{9,8},{10,9},{11,10},{12... | collective-permute-start | bytes 196616 | tf_op jit(solution)/shard_map/ppermute | solution.py:15
  229.9 2.4 slice-start.5
  239.2 18.2 %copy-start.2 = (bf16[1,16,8,8,512]{4,3,0,1,2:T(8,128)(2,1)S(1)}, bf16[1,16,8,8,512]{4,3,0,1,2:T(8,128)(2,1)}, u32[]{:S(2)}) copy-start(bf16[1,16,8,8,512]{4,3,0,1,2:T(8,128)(2,1)} %copy-done) | copy-start | bytes 3145732
  241.3 16.1 %collective-permute-start.16 = (bf16[16,64,512]{2,1,0:T(8,128)(2,1)S(1)}, bf16[16,64,512]{2,1,0:T(8,128)(2,1)S(1)}, u32[]{:S(2)}, u32[]{:S(2)}) collective-permute-start(bf16[16,64,512]{2,1,0:T(8,128)(2,1)S(1)} %get-tuple-element.8), channel_id=1, source_target_pairs={{0,8},{8,16},{16,24},{1,9},{9,17},{17,25},{2,10},{10,18},{18,26},{... | collective-permute-start | bytes 3145736 | tf_op jit(solution)/shard_map/ppermute | solution.py:23
  257.4 16.9 %slice-start.6 = ((s8[4718592]{0:T(1024)(128)(4,1)}), s8[524288]{0:T(1024)(128)(4,1)S(1)}, s32[]{:S(2)}) async-start(s8[4718592]{0:T(1024)(128)(4,1)} %bitcast.369), calls=%async_computation.8 | async-start | bytes 1048576
  259.4 6.4 %collective-permute-start.17 = (bf16[1,64,512]{2,1,0:T(8,128)(2,1)S(1)}, bf16[1,64,512]{2,1,0:T(8,128)(2,1)S(1)}, u32[]{:S(2)}, u32[]{:S(2)}) collective-permute-start(bf16[1,64,512]{2,1,0:T(8,128)(2,1)S(1)} %get-tuple-element.82), channel_id=1, source_target_pairs={{0,1},{1,2},{2,3},{3,4},{4,5},{5,6},{6,7},{8,9},{9,10},{10,11},{11... | collective-permute-start | bytes 196616 | tf_op jit(solution)/shard_map/ppermute | solution.py:12
  263.1 7.1 %collective-permute-start.18 = (bf16[1,64,512]{2,1,0:T(8,128)(2,1)S(1)}, bf16[1,64,512]{2,1,0:T(8,128)(2,1)S(1)}, u32[]{:S(2)}, u32[]{:S(2)}) collective-permute-start(bf16[1,64,512]{2,1,0:T(8,128)(2,1)S(1)} %get-tuple-element.83), channel_id=1, source_target_pairs={{1,0},{2,1},{3,2},{4,3},{5,4},{6,5},{7,6},{9,8},{10,9},{11,10},{12... | collective-permute-start | bytes 196616 | tf_op jit(solution)/shard_map/ppermute | solution.py:15
  271.8 2.4 slice-start.7
  281.1 18.2 %copy-start.3 = (bf16[1,16,8,8,512]{4,3,0,1,2:T(8,128)(2,1)S(1)}, bf16[1,16,8,8,512]{4,3,0,1,2:T(8,128)(2,1)}, u32[]{:S(2)}) copy-start(bf16[1,16,8,8,512]{4,3,0,1,2:T(8,128)(2,1)} %copy-done) | copy-start | bytes 3145732
  283.1 16.1 %collective-permute-start.19 = (bf16[16,64,512]{2,1,0:T(8,128)(2,1)S(1)}, bf16[16,64,512]{2,1,0:T(8,128)(2,1)S(1)}, u32[]{:S(2)}, u32[]{:S(2)}) collective-permute-start(bf16[16,64,512]{2,1,0:T(8,128)(2,1)S(1)} %get-tuple-element.6), channel_id=1, source_target_pairs={{0,8},{8,16},{16,24},{1,9},{9,17},{17,25},{2,10},{10,18},{18,26},{... | collective-permute-start | bytes 3145736 | tf_op jit(solution)/shard_map/ppermute | solution.py:23
  301.3 7.4 %collective-permute-start.20 = (bf16[1,64,512]{2,1,0:T(8,128)(2,1)S(1)}, bf16[1,64,512]{2,1,0:T(8,128)(2,1)S(1)}, u32[]{:S(2)}, u32[]{:S(2)}) collective-permute-start(bf16[1,64,512]{2,1,0:T(8,128)(2,1)S(1)} %get-tuple-element.80), channel_id=1, source_target_pairs={{0,1},{1,2},{2,3},{3,4},{4,5},{5,6},{6,7},{8,9},{9,10},{10,11},{11... | collective-permute-start | bytes 196616 | tf_op jit(solution)/shard_map/ppermute | solution.py:12
  305.2 7.1 %collective-permute-start.21 = (bf16[1,64,512]{2,1,0:T(8,128)(2,1)S(1)}, bf16[1,64,512]{2,1,0:T(8,128)(2,1)S(1)}, u32[]{:S(2)}, u32[]{:S(2)}) collective-permute-start(bf16[1,64,512]{2,1,0:T(8,128)(2,1)S(1)} %get-tuple-element.81), channel_id=1, source_target_pairs={{1,0},{2,1},{3,2},{4,3},{5,4},{6,5},{7,6},{9,8},{10,9},{11,10},{12... | collective-permute-start | bytes 196616 | tf_op jit(solution)/shard_map/ppermute | solution.py:15
  307.3 9.1 %slice-start.8 = ((s8[4718592]{0:T(1024)(128)(4,1)}), s8[4194304]{0:T(1024)(128)(4,1)S(1)}, s32[]{:S(2)}) async-start(s8[4718592]{0:T(1024)(128)(4,1)} %bitcast.380), calls=%async_computation.10 | async-start | bytes 8388608
  314.0 2.4 slice-start.9
Sparse Core Ops, SparseCore 0:
  64.7 21.8 all-gather.1
where the time goes:
time: 340 us; the launch traced here: 333 us
  waiting for transfers between devices  154 us (45%)
  starting transfers between devices  67.5 us (20%)
  matrix products  43.3 us (13%)
  other arithmetic  30.3 us (9%)
  local copies, waits for them, and re-layouts  23 us (7%)
  between operations  14.7 us (4%)
    ppermute x4, waiting for transfers between devices, passed_along(): lax.ppermute(value, axis, [(source, source + steps) for source in range(f...  57.1 us
    all_to_all x1, waiting for transfers between devices, shards(): lax.all_to_all(banded, 'strip', split_axis=1, concat_axis=2, tiled=True)  48.1 us
    dot_general x63, matrix products, conv_valid(): jnp.dot(window, weight[row_off, col_off], preferred_element_type=jnp.floa...  42.2 us
    ppermute x9, starting transfers between devices, padded_2(): lax.ppermute(lax.slice_in_dim(block, 0, width, axis=dim), axis, backward)  29.8 us
    ppermute x9, waiting for transfers between devices, padded_2(): lax.ppermute(lax.slice_in_dim(block, 0, width, axis=dim), axis, backward)  25.9 us
    ppermute x9, starting transfers between devices, padded_2(): lax.ppermute(lax.slice_in_dim(block, block.shape[dim] - width, None, axis...  24 us
    all_gather x1, waiting for transfers between devices, shards(): banded = lax.all_gather(reduced, 'segment', axis=1, tiled=True)  22 us
    slice x6, local copies, waits for them, and re-layouts, conv_valid(): padded[:, row_off:row_off + rows, col_off:col_off + columns, :]  12.7 us
  transfers between devices with their start and end apart: 24, of which 17 were waited for; matrix products, arithmetic and copies ran while one was open for 1% of the time, Pallas kernels for 0%

commit v1 on v0

v1 whole, which is shorter than its diff:
```python
import functools

import jax
import jax.numpy as jnp
import numpy as np
from jax import lax
from jax.experimental import pallas as pl
from jax.experimental.pallas import tpu as pltpu
from jax.sharding import PartitionSpec as P

MESH = pl.DeviceIdType.MESH
EDGE = 16
DIRS = [(dg, ds) for dg in (-1, 0, 1) for ds in (-1, 0, 1) if (dg, ds) != (0, 0)]


def fits(count, pitch, limit):
    best = 1
    for size in range(1, count + 1):
        if count % size == 0 and size * pitch <= limit:
            best = size
    return best


def kernel(
    dims,
    feat,
    wf,
    ws,
    wd,
    wsec,
    perm,
    out,
    x_buf,
    f_buf,
    s_buf,
    d_buf,
    r_buf,
    z_buf,
    o_buf,
    wf_v,
    ws_v,
    wd_v,
    wsec_v,
    wsem,
    fsem,
    hsend,
    hrecv,
    rsend,
    rmain,
    rtop,
    rbot,
    csend,
    crecv,
    esend,
    erecv,
    osem,
):
    S, N, B, R, C, K1, K2 = dims
    RD, CD = R // 2, C // 2
    m = N // S
    sr = RD // m
    cols = CD * N
    cr = max(1, 256 // cols)
    n = sr // cr
    pitch = R + 2 * EDGE
    g = lax.axis_index("segment")
    s = lax.axis_index("strip")

    copies = []
    for a in range(3):
        for c in range(3):
            copies.append(
                (0, wf.at[a, c], wf_v.at[pl.ds(c * K1, K1), pl.ds(a * K1, K1)])
            )
    for a in range(3):
        for c in range(3):
            copies.append(
                (1, ws.at[a, c], ws_v.at[pl.ds(c * K1, K1), pl.ds(a * K1, K1)])
            )
    for a in range(2):
        for c in range(2):
            copies.append((2, wd.at[a, c], wd_v.at[pl.ds((2 * a + c) * K1, K1)]))
    for a in range(3):
        for c in range(3):
            copies.append(
                (3, wsec.at[0, a, c], wsec_v.at[pl.ds(a * K2, K2), pl.ds(c * K2, K2)])
            )
    weights = [
        (group, pltpu.make_async_copy(src, dst, wsem.at[i]))
        for i, (group, src, dst) in enumerate(copies)
    ]

    def weights_wait(which):
        for group, copy in weights:
            if group == which:
                copy.wait()

    centre = [
        pltpu.make_async_copy(
            feat.at[b], x_buf.at[b, pl.ds(2, C), pl.ds(EDGE, R)], fsem.at[b]
        )
        for b in range(B)
    ]
    for copy in centre:
        copy.start()
    for _, copy in weights:
        copy.start()

    zero = jnp.bfloat16(0)
    x_buf[:, 0:2] = jnp.full((B, 2, pitch, K1), zero)
    x_buf[:, C + 2 : C + 4] = jnp.full((B, 2, pitch, K1), zero)
    x_buf[:, 2 : C + 2, 0:EDGE] = jnp.full((B, C, EDGE, K1), zero)
    x_buf[:, 2 : C + 2, EDGE + R :] = jnp.full((B, C, EDGE, K1), zero)
    z_buf[:, 0] = jnp.full((B, cols, K2), zero)
    z_buf[:, sr + 1] = jnp.full((B, cols, K2), zero)
    r_buf[:, :, 0 : 2 * CD] = jnp.full((B, N, 2 * CD, K2), zero)
    r_buf[:, :, (sr + 2) * CD :] = jnp.full((B, N, 2 * CD, K2), zero)

    barrier = pltpu.get_barrier_semaphore()
    total = S * N
    me = g * N + s

    def greet(k, carry):
        other = lax.rem(me + k, total)
        pl.semaphore_signal(
            barrier,
            inc=1,
            device_id=(lax.div(other, N), lax.rem(other, N)),
            device_id_type=MESH,
        )
        return carry

    lax.fori_loop(1, total, greet, 0)
    pl.semaphore_wait(barrier, total - 1)

    def inside(gg, ss):
        return (gg >= 0) & (gg < S) & (ss >= 0) & (ss < N)

    row_src = {-1: (0, EDGE), 0: (0, R), 1: (R - EDGE, EDGE)}
    row_dst = {-1: EDGE + R, 0: EDGE, 1: 0}
    col_src = {-1: (0, 2), 0: (0, C), 1: (C - 2, 2)}
    col_dst = {-1: C + 2, 0: 2, 1: 0}

    def border(b, i):
        dg, ds = DIRS[i]
        r0, rn = row_src[dg]
        c0, cn = col_src[ds]
        return pltpu.make_async_remote_copy(
            src_ref=feat.at[b, pl.ds(c0, cn), pl.ds(r0, rn)],
            dst_ref=x_buf.at[b, pl.ds(col_dst[ds], cn), pl.ds(row_dst[dg], rn)],
            send_sem=hsend.at[b, i],
            recv_sem=hrecv.at[b, i],
            device_id=(g + dg, s + ds),
            device_id_type=MESH,
        )

    for b in range(B):
        for i, (dg, ds) in enumerate(DIRS):

            @pl.when(inside(g + dg, s + ds))
            def _():
                border(b, i).start()

    def pieces(b):
        found = []
        for k in range(m):
            low, high = max(0, k * sr - 2), min(RD, k * sr + sr + 2)
            found.append(
                (
                    g * m + k,
                    True,
                    low,
                    high - low,
                    low - (k * sr - 2),
                    rmain,
                )
            )
        found.append((g * m - 1, g > 0, 0, 2, sr + 2, rbot))
        found.append((g * m + m, g < S - 1, RD - 2, 2, 0, rtop))
        made = []
        for i, (strip, active, low, count, at, sem) in enumerate(found):
            src = d_buf.at[b, pl.ds(low * CD, count * CD)]
            dst = r_buf.at[b, s, pl.ds(at * CD, count * CD)]
            remote = functools.partial(
                pltpu.make_async_remote_copy,
                src_ref=src,
                dst_ref=dst,
                send_sem=rsend.at[b, i],
                recv_sem=sem.at[b, s],
                device_id=(0, strip),
                device_id_type=MESH,
            )
            local = functools.partial(pltpu.make_async_copy, src, dst, sem.at[b, s])
            own = (g == 0) & (s == strip)
            made.append((active & ~own, active & own, remote, local))
        return made

    def conv_rows(buf, first_col, size, weight, sel):
        data = [
            buf[sel(first_col + j, size)].reshape(size * pitch, K1) for j in range(3)
        ]
        data = jnp.concatenate(data, axis=1)
        part = [
            jnp.dot(
                data,
                weight[:, a * K1 : (a + 1) * K1],
                preferred_element_type=jnp.float32,
            )
            for a in range(3)
        ]
        rows = size * pitch
        return pltpu.roll(part[0], 1, 0) + part[1] + pltpu.roll(part[2], rows - 1, 0)

    size1 = fits(C + 2, pitch, 320)
    size2 = fits(C, pitch, 400)

    def stem(b):
        centre[b].wait()
        for i, (dg, ds) in enumerate(DIRS):

            @pl.when(inside(g - dg, s - ds))
            def _():
                border(b, i).wait_recv()

        if b == 0:
            weights_wait(0)

        def one(t, carry):
            c0 = t * size1
            conv = conv_rows(
                x_buf, c0, size1, wf_v, lambda at, size: (b, pl.ds(at, size))
            )
            conv = conv.reshape(size1, pitch, K1)
            inner = x_buf[b, pl.ds(c0 + 1, size1)].astype(jnp.float32)
            value = jnp.maximum(inner + conv, 0.0)
            col = lax.broadcasted_iota(jnp.int32, (size1, pitch, K1), 0) + (
                s * C + c0 - 1
            )
            row = lax.broadcasted_iota(jnp.int32, (size1, pitch, K1), 1) + (g * R - EDGE)
            keep = (col >= 0) & (col < N * C) & (row >= 0) & (row < S * R)
            f_buf[pl.ds(c0, size1)] = jnp.where(keep, value, 0.0).astype(jnp.bfloat16)
            return carry

        lax.fori_loop(0, (C + 2) // size1, one, 0)
        if b == 0:
            weights_wait(1)

        def two(t, carry):
            c0 = t * size2
            conv = conv_rows(f_buf, c0, size2, ws_v, lambda at, size: (pl.ds(at, size),))
            conv = conv.reshape(size2, pitch, K1)[:, EDGE : EDGE + R]
            inner = f_buf[pl.ds(c0 + 1, size2), EDGE : EDGE + R].astype(jnp.float32)
            value = jnp.maximum(inner + conv, 0.0)
            at = pl.multiple_of(c0 * R, R)
            value = value.reshape(size2 * R, K1)
            for q in range(K1 // 128):
                s_buf[q, pl.ds(at, size2 * R), :] = value[:, q * 128 : (q + 1) * 128]
            return carry

        lax.fori_loop(0, C // size2, two, 0)
        if b == 0:
            weights_wait(2)
        taps = []
        for a in range(2):
            picked = jnp.concatenate(
                [
                    s_buf[q, pl.ds(a, C * RD, stride=2), :]
                    for q in range(K1 // 128)
                ],
                axis=1,
            )
            picked = picked.reshape(CD, 2, RD, K1)
            for c in range(2):
                taps.append(picked[:, c].reshape(CD * RD, K1).astype(jnp.bfloat16))
        reduced = jnp.dot(
            jnp.concatenate(taps, axis=1), wd_v[...], preferred_element_type=jnp.float32
        )
        reduced = jnp.maximum(reduced, 0.0).astype(jnp.bfloat16)
        d_buf[b] = jnp.dot(
            perm[...], reduced, preferred_element_type=jnp.float32
        ).astype(jnp.bfloat16)
        for away, home, remote, local in pieces(b):

            @pl.when(away)
            def _():
                remote().start()

            @pl.when(home)
            def _():
                local().start()

    for b in range(B):
        stem(b)
    weights_wait(3)

    def arrive(b):
        def waits(src, carry):
            for k in range(m):
                low, high = max(0, k * sr - 2), min(RD, k * sr + sr + 2)
                part = r_buf.at[
                    b, src, pl.ds((low - (k * sr - 2)) * CD, (high - low) * CD)
                ]

                @pl.when(lax.rem(s, m) == k)
                def _():
                    pltpu.make_async_copy(part, part, rmain.at[b, src]).wait()

            top = r_buf.at[b, src, pl.ds(0, 2 * CD)]
            bottom = r_buf.at[b, src, pl.ds((sr + 2) * CD, 2 * CD)]

            @pl.when((lax.rem(s, m) == 0) & (s > 0))
            def _():
                pltpu.make_async_copy(top, top, rtop.at[b, src]).wait()

            @pl.when((lax.rem(s, m) == m - 1) & (s < N - 1))
            def _():
                pltpu.make_async_copy(bottom, bottom, rbot.at[b, src]).wait()

            return carry

        lax.fori_loop(0, N, waits, 0)
        group = max(1, EDGE // CD)
        for q in range(N // group):
            parts = [
                r_buf[b, q * group + j]
                .astype(jnp.float32)
                .reshape(sr + 4, CD, K2)[1 : sr + 3]
                for j in range(group)
            ]
            whole = parts[0] if group == 1 else jnp.concatenate(parts, axis=1)
            z_buf[b, :, q * group * CD : (q + 1) * group * CD] = whole.astype(
                jnp.bfloat16
            )

    def chunk_copy(b, k):
        rows = pl.ds(k * cr, cr)
        return pltpu.make_async_remote_copy(
            src_ref=o_buf.at[b, rows],
            dst_ref=z_buf.at[b, pl.ds(k * cr + 1, cr)],
            send_sem=csend.at[b, k],
            recv_sem=crecv.at[b, k],
            device_id=(g + 1, s),
            device_id_type=MESH,
        )

    def edge_copy(b, low):
        src, dst, to = (0, sr + 1, s - 1) if low else (sr - 1, 0, s + 1)
        i = 0 if low else 1
        return pltpu.make_async_remote_copy(
            src_ref=o_buf.at[b, pl.ds(src, 1)],
            dst_ref=z_buf.at[b, pl.ds(dst, 1)],
            send_sem=esend.at[b, i],
            recv_sem=erecv.at[b, i],
            device_id=(g + 1, to),
            device_id_type=MESH,
        )

    def out_copy(b, k):
        rows = pl.ds(k * cr, cr)
        return pltpu.make_async_copy(
            o_buf.at[b, rows], out.at[0, b, rows], osem.at[b, k]
        )

    span = cr * cols
    width = 256

    def section(b, p):
        k = jnp.where(p == n - 1, n - 1, jnp.where(p == n - 2, 0, p + 1))

        @pl.when(g > 0)
        def _():
            @pl.when(p == 0)
            def _():
                for j in range(3):
                    chunk_copy(b, j).wait_recv()

            @pl.when((p > 0) & (p < n - 2))
            def _():
                chunk_copy(b, p + 2).wait_recv()

            @pl.when((p == n - 2) & (s > 0))
            def _():
                edge_copy(b, False).wait_recv()

            @pl.when((p == n - 1) & (s < N - 1))
            def _():
                edge_copy(b, True).wait_recv()

        data = jnp.concatenate(
            [z_buf[b, pl.ds(k * cr + a, cr)].reshape(span, K2) for a in range(3)],
            axis=1,
        )
        place = lax.broadcasted_iota(jnp.int32, (cr, cols, width), 1).reshape(span, width)
        for q in range(K2 // width):
            part = [
                jnp.dot(
                    data,
                    wsec_v[:, c * K2 + q * width : c * K2 + (q + 1) * width],
                    preferred_element_type=jnp.float32,
                )
                for c in range(3)
            ]
            left = jnp.where(place == 0, 0.0, pltpu.roll(part[0], 1, 0))
            right = jnp.where(place == cols - 1, 0.0, pltpu.roll(part[2], span - 1, 0))
            inner = z_buf[
                b, pl.ds(k * cr + 1, cr), :, q * width : (q + 1) * width
            ].reshape(span, width)
            value = jnp.maximum(inner.astype(jnp.float32) + left + part[1] + right, 0.0)
            o_buf[b, pl.ds(k * cr, cr), :, q * width : (q + 1) * width] = value.astype(
                jnp.bfloat16
            ).reshape(cr, cols, width)
        out_copy(b, k).start()

        @pl.when(g < S - 1)
        def _():
            @pl.when((k == 0) & (s > 0))
            def _():
                edge_copy(b, True).start()

            @pl.when((k == n - 1) & (s < N - 1))
            def _():
                edge_copy(b, False).start()

            chunk_copy(b, k).start()

    for b in range(B):

        @pl.when(g == 0)
        def _():
            arrive(b)

        def step(p, carry):
            section(b, p)
            return carry

        lax.fori_loop(0, n, step, 0)

    for b in range(B):
        for i, (dg, ds) in enumerate(DIRS):

            @pl.when(inside(g + dg, s + ds))
            def _():
                border(b, i).wait_send()

        for away, home, remote, local in pieces(b):

            @pl.when(away)
            def _():
                remote().wait_send()

        @pl.when(g < S - 1)
        def _():
            @pl.when(s > 0)
            def _():
                edge_copy(b, True).wait_send()

            @pl.when(s < N - 1)
            def _():
                edge_copy(b, False).wait_send()

            for k in range(n):
                chunk_copy(b, k).wait_send()

        for k in range(n):
            out_copy(b, k).wait()


def shards(S, N, features, weight_first, weight_second, weight_down, section_weights):
    B, R, C, K1 = features.shape
    K2 = weight_down.shape[3]
    RD, CD = R // 2, C // 2
    m = N // S
    sr = RD // m
    cols = CD * N
    n = sr // max(1, 256 // cols)
    pitch = R + 2 * EDGE
    p = np.arange(RD * CD)
    perm = (np.arange(RD * CD)[None, :] == ((p % CD) * RD + p // CD)[:, None])
    perm = jnp.asarray(perm, jnp.bfloat16)
    bf16, f32 = jnp.bfloat16, jnp.float32
    dma = pltpu.SemaphoreType.DMA
    anywhere = pl.BlockSpec(memory_space=pl.ANY)
    flops = 2 * B * (R * C * 18 * K1 * K1 + RD * CD * 4 * K1 * K2 + sr * cols * 9 * K2 * K2)
    return pl.pallas_call(
        functools.partial(kernel, (S, N, B, R, C, K1, K2)),
        out_shape=jax.ShapeDtypeStruct((1, B, sr, cols, K2), bf16),
        in_specs=[anywhere] * 5 + [pl.BlockSpec(memory_space=pltpu.VMEM)],
        out_specs=anywhere,
        scratch_shapes=[
            pltpu.VMEM((B, C + 4, pitch, K1), bf16),
            pltpu.VMEM((C + 2, pitch, K1), bf16),
            pltpu.VMEM((K1 // 128, C * R, 128), f32),
            pltpu.VMEM((B, RD * CD, K2), bf16),
            pltpu.VMEM((B, N, (sr + 4) * CD, K2), bf16),
            pltpu.VMEM((B, sr + 2, cols, K2), bf16),
            pltpu.VMEM((B, sr, cols, K2), bf16),
            pltpu.VMEM((3 * K1, 3 * K1), bf16),
            pltpu.VMEM((3 * K1, 3 * K1), bf16),
            pltpu.VMEM((4 * K1, K2), bf16),
            pltpu.VMEM((3 * K2, 3 * K2), bf16),
            dma((31,)),
            dma((B,)),
            dma((B, 8)),
            dma((B, 8)),
            dma((B, m + 2)),
            dma((B, N)),
            dma((B, N)),
            dma((B, N)),
            dma((B, n)),
            dma((B, n)),
            dma((B, 2)),
            dma((B, 2)),
            dma((B, n)),
        ],
        compiler_params=pltpu.CompilerParams(
            collective_id=0, has_side_effects=True, vmem_limit_bytes=56 * 1024 * 1024
        ),
        cost_estimate=pl.CostEstimate(
            flops=flops, bytes_accessed=16 * 1024 * 1024, transcendentals=0
        ),
    )(
        jnp.transpose(features, (0, 2, 1, 3)),
        weight_first,
        weight_second,
        weight_down,
        section_weights,
        perm,
    )


def solution(mesh):
    return jax.shard_map(
        functools.partial(shards, mesh.shape["segment"], mesh.shape["strip"]),
        mesh=mesh,
        in_specs=(
            P(None, "segment", "strip", None),
            P(),
            P(),
            P(),
            P("segment", None, None, None, None),
        ),
        out_specs=P("segment", None, "strip", None, None),
        check_vma=False,
    )
```

time: 340 us -> 93.9 us (0.28)
  the two profiles are of different devices: /device:TPU:6 before, /device:TPU:11 now
where the time goes in v1:
time: 93.9 us; the launch traced here: 93.5 us
  Pallas kernels  87.8 us (94%)
  local copies, waits for them, and re-layouts  5.67 us (6%)
    pallas_call x1, Pallas kernels, shards(): pl.pallas_call(functools.partial(kernel, (S, N, B, R, C, K1, K2)), out_sh...  87.8 us
    unnamed x2, local copies, waits for them, and re-layouts  5.67 us

profile of v1, /device:TPU:11, one launch (start us, length us, event | category | flops | bytes accessed | tf_op | source)
XLA Modules:
  0.0 93.5 jit_solution(17448757874816291752)
XLA Ops:
  0.0 2.5 %copy.9 = bf16[2,64,16,256]{3,1,2,0:T(8,128)(2,1)} copy(bf16[2,64,16,256]{3,2,1,0:T(8,128)(2,1)} %param.6) | data formatting | bytes 2097152 | tf_op args[0]
  2.5 87.8 %shard_map.64 = bf16[1,2,16,64,512]{4,3,2,1,0:T(8,128)(2,1)} custom-call(bf16[2,16,64,256]{3,2,1,0:T(8,128)(2,1)} %bitcast.3, bf16[3,3,256,256]{3,2,1,0:T(8,128)(2,1)} %wf.1, bf16[3,3,256,256]{3,2,1,0:T(8,128)(2,1)} %ws.1, bf16[2,2,256,512]{3,2,1,0:T(8,128)(2,1)} %wd.1, bf16[1,3,3,512,512]{4,3,2,1,0:T(8,128)(2,1)} %wsec.1, bf16[256,256]{1,0:T(8,128)(2,1)} %constant.2.clone.perm), custom_call_target="tpu_custom_call" | custom-call | flops 15032385536 | bytes 16777216 | tf_op jit(solution)/shard_map/pallas_call | solution.py:484
  90.4 3.1 %copy.11 = bf16[1,2,16,64,512]{4,3,2,1,0:T(8,128)(2,1)} copy(bf16[1,2,16,64,512]{4,3,2,1,0:T(8,128)(2,1)} %shard_map.64) | data formatting | bytes 4194304

commit v2 on v1

--- a/solution.py
+++ b/solution.py
@@ -2,7 +2,6 @@
 
 import jax
 import jax.numpy as jnp
-import numpy as np
 from jax import lax
 from jax.experimental import pallas as pl
 from jax.experimental.pallas import tpu as pltpu
@@ -28,8 +27,10 @@
     ws,
     wd,
     wsec,
-    perm,
     out,
+    raw_buf,
+    top_buf,
+    bot_buf,
     x_buf,
     f_buf,
     s_buf,
@@ -47,10 +48,9 @@
     hrecv,
     rsend,
     rmain,
-    rtop,
-    rbot,
     csend,
     crecv,
+    zsend,
     esend,
     erecv,
     osem,
@@ -62,7 +62,7 @@
     cols = CD * N
     cr = max(1, 256 // cols)
     n = sr // cr
-    pitch = R + 2 * EDGE
+    pitch = R + EDGE
     g = lax.axis_index("segment")
     s = lax.axis_index("strip")
 
@@ -97,7 +97,7 @@
 
     centre = [
         pltpu.make_async_copy(
-            feat.at[b], x_buf.at[b, pl.ds(2, C), pl.ds(EDGE, R)], fsem.at[b]
+            feat.at[b], raw_buf.at[b], fsem.at[b]
         )
         for b in range(B)
     ]
@@ -109,12 +109,26 @@
     zero = jnp.bfloat16(0)
     x_buf[:, 0:2] = jnp.full((B, 2, pitch, K1), zero)
     x_buf[:, C + 2 : C + 4] = jnp.full((B, 2, pitch, K1), zero)
-    x_buf[:, 2 : C + 2, 0:EDGE] = jnp.full((B, C, EDGE, K1), zero)
-    x_buf[:, 2 : C + 2, EDGE + R :] = jnp.full((B, C, EDGE, K1), zero)
+    top_buf[...] = jnp.full((B, C + 4, EDGE, K1), zero)
+    bot_buf[...] = jnp.full((B, C + 4, EDGE, K1), zero)
     z_buf[:, 0] = jnp.full((B, cols, K2), zero)
     z_buf[:, sr + 1] = jnp.full((B, cols, K2), zero)
-    r_buf[:, :, 0 : 2 * CD] = jnp.full((B, N, 2 * CD, K2), zero)
-    r_buf[:, :, (sr + 2) * CD :] = jnp.full((B, N, 2 * CD, K2), zero)
+
+    def swap(outer, inner):
+        shape = (inner, outer, outer * inner)
+        i, j, q = [lax.broadcasted_iota(jnp.int32, shape, d) for d in range(3)]
+        hot = jnp.where(q == j * inner + i, 1.0, 0.0)
+        return hot.reshape(outer * inner, outer * inner).astype(jnp.bfloat16)
+
+    turn = swap(EDGE, C)
+    for b in range(B):
+        centre[b].wait()
+        for q in range(R // EDGE):
+            block = raw_buf[b, q * EDGE : (q + 1) * EDGE].reshape(EDGE * C, K1)
+            block = jnp.dot(turn, block, preferred_element_type=jnp.float32)
+            x_buf[b, 2 : C + 2, q * EDGE : (q + 1) * EDGE] = block.astype(
+                jnp.bfloat16
+            ).reshape(C, EDGE, K1)
 
     barrier = pltpu.get_barrier_semaphore()
     total = S * N
@@ -137,17 +151,21 @@
         return (gg >= 0) & (gg < S) & (ss >= 0) & (ss < N)
 
     row_src = {-1: (0, EDGE), 0: (0, R), 1: (R - EDGE, EDGE)}
-    row_dst = {-1: EDGE + R, 0: EDGE, 1: 0}
-    col_src = {-1: (0, 2), 0: (0, C), 1: (C - 2, 2)}
+    col_src = {-1: (2, 2), 0: (2, C), 1: (C, 2)}
     col_dst = {-1: C + 2, 0: 2, 1: 0}
 
     def border(b, i):
         dg, ds = DIRS[i]
         r0, rn = row_src[dg]
         c0, cn = col_src[ds]
+        where = pl.ds(col_dst[ds], cn)
+        if dg == 0:
+            dst = x_buf.at[b, where, pl.ds(0, R)]
+        else:
+            dst = (top_buf if dg == 1 else bot_buf).at[b, where]
         return pltpu.make_async_remote_copy(
-            src_ref=feat.at[b, pl.ds(c0, cn), pl.ds(r0, rn)],
-            dst_ref=x_buf.at[b, pl.ds(col_dst[ds], cn), pl.ds(row_dst[dg], rn)],
+            src_ref=x_buf.at[b, pl.ds(c0, cn), pl.ds(r0, rn)],
+            dst_ref=dst,
             send_sem=hsend.at[b, i],
             recv_sem=hrecv.at[b, i],
             device_id=(g + dg, s + ds),
@@ -162,37 +180,23 @@
                 border(b, i).start()
 
     def pieces(b):
-        found = []
+        made = []
         for k in range(m):
-            low, high = max(0, k * sr - 2), min(RD, k * sr + sr + 2)
-            found.append(
-                (
-                    g * m + k,
-                    True,
-                    low,
-                    high - low,
-                    low - (k * sr - 2),
-                    rmain,
-                )
-            )
-        found.append((g * m - 1, g > 0, 0, 2, sr + 2, rbot))
-        found.append((g * m + m, g < S - 1, RD - 2, 2, 0, rtop))
-        made = []
-        for i, (strip, active, low, count, at, sem) in enumerate(found):
-            src = d_buf.at[b, pl.ds(low * CD, count * CD)]
-            dst = r_buf.at[b, s, pl.ds(at * CD, count * CD)]
+            strip = g * m + k
+            src = d_buf.at[b, pl.ds(k * sr * CD, sr * CD)]
+            dst = r_buf.at[b, s]
             remote = functools.partial(
                 pltpu.make_async_remote_copy,
                 src_ref=src,
                 dst_ref=dst,
-                send_sem=rsend.at[b, i],
-                recv_sem=sem.at[b, s],
+                send_sem=rsend.at[b, k],
+                recv_sem=rmain.at[b, s],
                 device_id=(0, strip),
                 device_id_type=MESH,
             )
-            local = functools.partial(pltpu.make_async_copy, src, dst, sem.at[b, s])
+            local = functools.partial(pltpu.make_async_copy, src, dst, rmain.at[b, s])
             own = (g == 0) & (s == strip)
-            made.append((active & ~own, active & own, remote, local))
+            made.append((~own, own, remote, local))
         return made
 
     def conv_rows(buf, first_col, size, weight, sel):
@@ -208,20 +212,23 @@
             )
             for a in range(3)
         ]
-        rows = size * pitch
-        return pltpu.roll(part[0], 1, 0) + part[1] + pltpu.roll(part[2], rows - 1, 0)
+        part = [p.reshape(size, pitch, K1) for p in part]
+        return pltpu.roll(part[0], 1, 1) + part[1] + pltpu.roll(part[2], pitch - 1, 1)
 
     size1 = fits(C + 2, pitch, 320)
     size2 = fits(C, pitch, 400)
 
     def stem(b):
-        centre[b].wait()
         for i, (dg, ds) in enumerate(DIRS):
 
             @pl.when(inside(g - dg, s - ds))
             def _():
                 border(b, i).wait_recv()
 
+        low = lax.broadcasted_iota(jnp.int32, (C + 4, EDGE, K1), 1) < EDGE // 2
+        x_buf[b, :, R:] = jnp.where(
+            low, bot_buf[b].astype(jnp.float32), top_buf[b].astype(jnp.float32)
+        ).astype(jnp.bfloat16)
         if b == 0:
             weights_wait(0)
 
@@ -230,13 +237,13 @@
             conv = conv_rows(
                 x_buf, c0, size1, wf_v, lambda at, size: (b, pl.ds(at, size))
             )
-            conv = conv.reshape(size1, pitch, K1)
             inner = x_buf[b, pl.ds(c0 + 1, size1)].astype(jnp.float32)
             value = jnp.maximum(inner + conv, 0.0)
             col = lax.broadcasted_iota(jnp.int32, (size1, pitch, K1), 0) + (
                 s * C + c0 - 1
             )
-            row = lax.broadcasted_iota(jnp.int32, (size1, pitch, K1), 1) + (g * R - EDGE)
+            row = lax.broadcasted_iota(jnp.int32, (size1, pitch, K1), 1)
+            row = jnp.where(row < R + EDGE // 2, row, row - pitch) + g * R
             keep = (col >= 0) & (col < N * C) & (row >= 0) & (row < S * R)
             f_buf[pl.ds(c0, size1)] = jnp.where(keep, value, 0.0).astype(jnp.bfloat16)
             return carry
@@ -248,8 +255,8 @@
         def two(t, carry):
             c0 = t * size2
             conv = conv_rows(f_buf, c0, size2, ws_v, lambda at, size: (pl.ds(at, size),))
-            conv = conv.reshape(size2, pitch, K1)[:, EDGE : EDGE + R]
-            inner = f_buf[pl.ds(c0 + 1, size2), EDGE : EDGE + R].astype(jnp.float32)
+            conv = conv[:, :R]
+            inner = f_buf[pl.ds(c0 + 1, size2), :R].astype(jnp.float32)
             value = jnp.maximum(inner + conv, 0.0)
             at = pl.multiple_of(c0 * R, R)
             value = value.reshape(size2 * R, K1)
@@ -277,7 +284,7 @@
         )
         reduced = jnp.maximum(reduced, 0.0).astype(jnp.bfloat16)
         d_buf[b] = jnp.dot(
-            perm[...], reduced, preferred_element_type=jnp.float32
+            swap(CD, RD), reduced, preferred_element_type=jnp.float32
         ).astype(jnp.bfloat16)
         for away, home, remote, local in pieces(b):
 
@@ -293,44 +300,43 @@
         stem(b)
     weights_wait(3)
 
+    def strip_copy(b, low):
+        src, dst, to = (1, sr + 1, s - 1) if low else (sr, 0, s + 1)
+        i = 0 if low else 1
+        return pltpu.make_async_remote_copy(
+            src_ref=z_buf.at[b, pl.ds(src, 1)],
+            dst_ref=z_buf.at[b, pl.ds(dst, 1)],
+            send_sem=zsend.at[b, i],
+            recv_sem=erecv.at[b, i],
+            device_id=(g, to),
+            device_id_type=MESH,
+        )
+
     def arrive(b):
         def waits(src, carry):
-            for k in range(m):
-                low, high = max(0, k * sr - 2), min(RD, k * sr + sr + 2)
-                part = r_buf.at[
-                    b, src, pl.ds((low - (k * sr - 2)) * CD, (high - low) * CD)
-                ]
-
-                @pl.when(lax.rem(s, m) == k)
-                def _():
-                    pltpu.make_async_copy(part, part, rmain.at[b, src]).wait()
-
-            top = r_buf.at[b, src, pl.ds(0, 2 * CD)]
-            bottom = r_buf.at[b, src, pl.ds((sr + 2) * CD, 2 * CD)]
-
-            @pl.when((lax.rem(s, m) == 0) & (s > 0))
-            def _():
-                pltpu.make_async_copy(top, top, rtop.at[b, src]).wait()
-
-            @pl.when((lax.rem(s, m) == m - 1) & (s < N - 1))
-            def _():
-                pltpu.make_async_copy(bottom, bottom, rbot.at[b, src]).wait()
-
+            part = r_buf.at[b, src]
+            pltpu.make_async_copy(part, part, rmain.at[b, src]).wait()
             return carry
 
         lax.fori_loop(0, N, waits, 0)
         group = max(1, EDGE // CD)
         for q in range(N // group):
             parts = [
-                r_buf[b, q * group + j]
-                .astype(jnp.float32)
-                .reshape(sr + 4, CD, K2)[1 : sr + 3]
+                r_buf[b, q * group + j].astype(jnp.float32).reshape(sr, CD, K2)
                 for j in range(group)
             ]
             whole = parts[0] if group == 1 else jnp.concatenate(parts, axis=1)
-            z_buf[b, :, q * group * CD : (q + 1) * group * CD] = whole.astype(
+            z_buf[b, 1 : sr + 1, q * group * CD : (q + 1) * group * CD] = whole.astype(
                 jnp.bfloat16
             )
+
+        @pl.when(s > 0)
+        def _():
+            strip_copy(b, True).start()
+
+        @pl.when(s < N - 1)
+        def _():
+            strip_copy(b, False).start()
 
     def chunk_copy(b, k):
         rows = pl.ds(k * cr, cr)
@@ -378,13 +384,13 @@
             def _():
                 chunk_copy(b, p + 2).wait_recv()
 
-            @pl.when((p == n - 2) & (s > 0))
-            def _():
-                edge_copy(b, False).wait_recv()
-
-            @pl.when((p == n - 1) & (s < N - 1))
-            def _():
-                edge_copy(b, True).wait_recv()
+        @pl.when((p == n - 2) & (s > 0))
+        def _():
+            edge_copy(b, False).wait_recv()
+
+        @pl.when((p == n - 1) & (s < N - 1))
+        def _():
+            edge_copy(b, True).wait_recv()
 
         data = jnp.concatenate(
             [z_buf[b, pl.ds(k * cr + a, cr)].reshape(span, K2) for a in range(3)],
@@ -448,6 +454,14 @@
             def _():
                 remote().wait_send()
 
+        @pl.when((g == 0) & (s > 0))
+        def _():
+            strip_copy(b, True).wait_send()
+
+        @pl.when((g == 0) & (s < N - 1))
+        def _():
+            strip_copy(b, False).wait_send()
+
         @pl.when(g < S - 1)
         def _():
             @pl.when(s > 0)
@@ -473,10 +487,7 @@
     sr = RD // m
     cols = CD * N
     n = sr // max(1, 256 // cols)
-    pitch = R + 2 * EDGE
-    p = np.arange(RD * CD)
-    perm = (np.arange(RD * CD)[None, :] == ((p % CD) * RD + p // CD)[:, None])
-    perm = jnp.asarray(perm, jnp.bfloat16)
+    pitch = R + EDGE
     bf16, f32 = jnp.bfloat16, jnp.float32
     dma = pltpu.SemaphoreType.DMA
     anywhere = pl.BlockSpec(memory_space=pl.ANY)
@@ -484,14 +495,17 @@
     return pl.pallas_call(
         functools.partial(kernel, (S, N, B, R, C, K1, K2)),
         out_shape=jax.ShapeDtypeStruct((1, B, sr, cols, K2), bf16),
-        in_specs=[anywhere] * 5 + [pl.BlockSpec(memory_space=pltpu.VMEM)],
+        in_specs=[pl.BlockSpec(memory_space=pltpu.HBM)] * 5,
         out_specs=anywhere,
         scratch_shapes=[
+            pltpu.VMEM((B, R, C, K1), bf16),
+            pltpu.VMEM((B, C + 4, EDGE, K1), bf16),
+            pltpu.VMEM((B, C + 4, EDGE, K1), bf16),
             pltpu.VMEM((B, C + 4, pitch, K1), bf16),
             pltpu.VMEM((C + 2, pitch, K1), bf16),
             pltpu.VMEM((K1 // 128, C * R, 128), f32),
             pltpu.VMEM((B, RD * CD, K2), bf16),
-            pltpu.VMEM((B, N, (sr + 4) * CD, K2), bf16),
+            pltpu.VMEM((B, N, sr * CD, K2), bf16),
             pltpu.VMEM((B, sr + 2, cols, K2), bf16),
             pltpu.VMEM((B, sr, cols, K2), bf16),
             pltpu.VMEM((3 * K1, 3 * K1), bf16),
@@ -502,12 +516,11 @@
             dma((B,)),
             dma((B, 8)),
             dma((B, 8)),
-            dma((B, m + 2)),
-            dma((B, N)),
-            dma((B, N)),
+            dma((B, m)),
             dma((B, N)),
             dma((B, n)),
             dma((B, n)),
+            dma((B, 2)),
             dma((B, 2)),
             dma((B, 2)),
             dma((B, n)),
@@ -519,12 +532,11 @@
             flops=flops, bytes_accessed=16 * 1024 * 1024, transcendentals=0
         ),
     )(
-        jnp.transpose(features, (0, 2, 1, 3)),
+        features,
         weight_first,
         weight_second,
         weight_down,
         section_weights,
-        perm,
     )
 
 

time: 93.9 us -> 91.5 us (0.974)
  local copies, waits for them, and re-layouts: 5.67 us -> 3.13 us
    unnamed x2 -> x1, local copies, waits for them, and re-layouts: 5.67 us -> 3.13 us
where the time goes in v2:
time: 91.5 us; the launch traced here: 91.3 us
  Pallas kernels  88.2 us (96%)
  local copies, waits for them, and re-layouts  3.13 us (3%)
    pallas_call x1, Pallas kernels, shards(): pl.pallas_call(functools.partial(kernel, (S, N, B, R, C, K1, K2)), out_sh...  88.2 us
    unnamed x1, local copies, waits for them, and re-layouts  3.13 us

profile of v2, /device:TPU:11, one launch (start us, length us, event | category | flops | bytes accessed | tf_op | source)
XLA Modules:
  0.0 91.3 jit_solution(3060932356952532473)
XLA Ops:
  0.0 88.2 %shard_map.55 = bf16[1,2,16,64,512]{4,3,2,1,0:T(8,128)(2,1)} custom-call(bf16[2,64,16,256]{3,2,1,0:T(8,128)(2,1)} %feat.1, bf16[3,3,256,256]{3,2,1,0:T(8,128)(2,1)} %wf.1, bf16[3,3,256,256]{3,2,1,0:T(8,128)(2,1)} %ws.1, bf16[2,2,256,512]{3,2,1,0:T(8,128)(2,1)} %wd.1, bf16[1,3,3,512,512]{4,3,2,1,0:T(8,128)(2,1)} %wsec.1), custom_call_target="tpu_custom_call" | custom-call | flops 15032385536 | bytes 16777216 | tf_op jit(solution)/shard_map/pallas_call | solution.py:495
  88.2 3.1 %copy.7 = bf16[1,2,16,64,512]{4,3,2,1,0:T(8,128)(2,1)} copy(bf16[1,2,16,64,512]{4,3,2,1,0:T(8,128)(2,1)} %shard_map.55) | data formatting | bytes 4194304

commit v3 on v2

--- a/solution.py
+++ b/solution.py
@@ -60,7 +60,7 @@
     m = N // S
     sr = RD // m
     cols = CD * N
-    cr = max(1, 256 // cols)
+    cr = max(1, 128 // cols)
     n = sr // cr
     pitch = R + EDGE
     g = lax.axis_index("segment")
@@ -486,7 +486,7 @@
     m = N // S
     sr = RD // m
     cols = CD * N
-    n = sr // max(1, 256 // cols)
+    n = sr // max(1, 128 // cols)
     pitch = R + EDGE
     bf16, f32 = jnp.bfloat16, jnp.float32
     dma = pltpu.SemaphoreType.DMA

time: 91.5 us -> 92.6 us (1.012)
  no operation moved by 1% of the time
where the time goes in v3:
time: 92.6 us; the launch traced here: 91.6 us
  Pallas kernels  88.4 us (95%)
  local copies, waits for them, and re-layouts  3.13 us (3%)
    pallas_call x1, Pallas kernels, shards(): pl.pallas_call(functools.partial(kernel, (S, N, B, R, C, K1, K2)), out_sh...  88.4 us
    unnamed x1, local copies, waits for them, and re-layouts  3.13 us

profile of v3, /device:TPU:11, one launch (start us, length us, event | category | flops | bytes accessed | tf_op | source)
XLA Modules:
  0.0 91.6 jit_solution(9397627444979442994)
XLA Ops:
  0.0 88.4 %shard_map.55 = bf16[1,2,16,64,512]{4,3,2,1,0:T(8,128)(2,1)} custom-call(bf16[2,64,16,256]{3,2,1,0:T(8,128)(2,1)} %feat.1, bf16[3,3,256,256]{3,2,1,0:T(8,128)(2,1)} %wf.1, bf16[3,3,256,256]{3,2,1,0:T(8,128)(2,1)} %ws.1, bf16[2,2,256,512]{3,2,1,0:T(8,128)(2,1)} %wd.1, bf16[1,3,3,512,512]{4,3,2,1,0:T(8,128)(2,1)} %wsec.1), custom_call_target="tpu_custom_call" | custom-call | flops 15032385536 | bytes 16777216 | tf_op jit(solution)/shard_map/pallas_call | solution.py:495
  88.4 3.1 %copy.7 = bf16[1,2,16,64,512]{4,3,2,1,0:T(8,128)(2,1)} copy(bf16[1,2,16,64,512]{4,3,2,1,0:T(8,128)(2,1)} %shard_map.55) | data formatting | bytes 4194304

commit v4 on v2

--- a/solution.py
+++ b/solution.py
@@ -286,6 +286,13 @@
         d_buf[b] = jnp.dot(
             swap(CD, RD), reduced, preferred_element_type=jnp.float32
         ).astype(jnp.bfloat16)
+        if b > 0:
+            for away, home, remote, local in pieces(b - 1):
+
+                @pl.when(away)
+                def _():
+                    remote().wait_send()
+
         for away, home, remote, local in pieces(b):
 
             @pl.when(away)
@@ -370,8 +377,11 @@
     span = cr * cols
     width = 256
 
+    def order(p):
+        return jnp.where(p == n - 1, n - 1, jnp.where(p == n - 2, 0, p + 1))
+
     def section(b, p):
-        k = jnp.where(p == n - 1, n - 1, jnp.where(p == n - 2, 0, p + 1))
+        k = order(p)
 
         @pl.when(g > 0)
         def _():
@@ -427,6 +437,16 @@
             def _():
                 edge_copy(b, False).start()
 
+            @pl.when(p >= 2)
+            def _():
+                chunk_copy(b, order(p - 2)).wait_send()
+
+            if b > 0:
+
+                @pl.when(p < 2)
+                def _():
+                    chunk_copy(b - 1, order(p + n - 2)).wait_send()
+
             chunk_copy(b, k).start()
 
     for b in range(B):
@@ -448,11 +468,12 @@
             def _():
                 border(b, i).wait_send()
 
-        for away, home, remote, local in pieces(b):
-
-            @pl.when(away)
-            def _():
-                remote().wait_send()
+        if b == B - 1:
+            for away, home, remote, local in pieces(b):
+
+                @pl.when(away)
+                def _():
+                    remote().wait_send()
 
         @pl.when((g == 0) & (s > 0))
         def _():
@@ -472,8 +493,9 @@
             def _():
                 edge_copy(b, False).wait_send()
 
-            for k in range(n):
-                chunk_copy(b, k).wait_send()
+            if b == B - 1:
+                chunk_copy(b, 0).wait_send()
+                chunk_copy(b, n - 1).wait_send()
 
         for k in range(n):
             out_copy(b, k).wait()

time: 91.5 us -> 91.4 us (level)
  no operation moved by 1% of the time
where the time goes in v4:
time: 91.4 us; the launch traced here: 91.3 us
  Pallas kernels  88.1 us (96%)
  local copies, waits for them, and re-layouts  3.13 us (3%)
    pallas_call x1, Pallas kernels, shards(): pl.pallas_call(functools.partial(kernel, (S, N, B, R, C, K1, K2)), out_sh...  88.1 us
    unnamed x1, local copies, waits for them, and re-layouts  3.13 us

profile of v4, /device:TPU:11, one launch (start us, length us, event | category | flops | bytes accessed | tf_op | source)
XLA Modules:
  0.0 91.3 jit_solution(13910911462005351771)
XLA Ops:
  0.0 88.1 %shard_map.55 = bf16[1,2,16,64,512]{4,3,2,1,0:T(8,128)(2,1)} custom-call(bf16[2,64,16,256]{3,2,1,0:T(8,128)(2,1)} %feat.1, bf16[3,3,256,256]{3,2,1,0:T(8,128)(2,1)} %wf.1, bf16[3,3,256,256]{3,2,1,0:T(8,128)(2,1)} %ws.1, bf16[2,2,256,512]{3,2,1,0:T(8,128)(2,1)} %wd.1, bf16[1,3,3,512,512]{4,3,2,1,0:T(8,128)(2,1)} %wsec.1), custom_call_target="tpu_custom_call" | custom-call | flops 15032385536 | bytes 16777216 | tf_op jit(solution)/shard_map/pallas_call | solution.py:517
  88.2 3.1 %copy.7 = bf16[1,2,16,64,512]{4,3,2,1,0:T(8,128)(2,1)} copy(bf16[1,2,16,64,512]{4,3,2,1,0:T(8,128)(2,1)} %shard_map.55) | data formatting | bytes 4194304

commit v5 on v4

--- a/solution.py
+++ b/solution.py
@@ -114,6 +114,28 @@
     z_buf[:, 0] = jnp.full((B, cols, K2), zero)
     z_buf[:, sr + 1] = jnp.full((B, cols, K2), zero)
 
+    def inside(gg, ss):
+        return (gg >= 0) & (gg < S) & (ss >= 0) & (ss < N)
+
+    barrier = pltpu.get_barrier_semaphore()
+    due = jnp.int32(0)
+    partners = [(g + dg, s + ds, inside(g + dg, s + ds)) for dg, ds in DIRS]
+    for k in range(m):
+        strip = g * m + k
+        partners.append((jnp.int32(0), strip, ~((g == 0) & (s == strip))))
+    for src in range(N):
+        band = lax.div(s, m)
+        away = ~((band == 0) & (s == src))
+        partners.append((band, jnp.int32(src), (g == 0) & away))
+    for gg, ss, there in partners:
+        due = due + jnp.where(there, 1, 0)
+
+        @pl.when(there)
+        def _():
+            pl.semaphore_signal(
+                barrier, inc=1, device_id=(gg, ss), device_id_type=MESH
+            )
+
     def swap(outer, inner):
         shape = (inner, outer, outer * inner)
         i, j, q = [lax.broadcasted_iota(jnp.int32, shape, d) for d in range(3)]
@@ -130,25 +152,7 @@
                 jnp.bfloat16
             ).reshape(C, EDGE, K1)
 
-    barrier = pltpu.get_barrier_semaphore()
-    total = S * N
-    me = g * N + s
-
-    def greet(k, carry):
-        other = lax.rem(me + k, total)
-        pl.semaphore_signal(
-            barrier,
-            inc=1,
-            device_id=(lax.div(other, N), lax.rem(other, N)),
-            device_id_type=MESH,
-        )
-        return carry
-
-    lax.fori_loop(1, total, greet, 0)
-    pl.semaphore_wait(barrier, total - 1)
-
-    def inside(gg, ss):
-        return (gg >= 0) & (gg < S) & (ss >= 0) & (ss < N)
+    pl.semaphore_wait(barrier, due)
 
     row_src = {-1: (0, EDGE), 0: (0, R), 1: (R - EDGE, EDGE)}
     col_src = {-1: (2, 2), 0: (2, C), 1: (C, 2)}
@@ -215,8 +219,8 @@
         part = [p.reshape(size, pitch, K1) for p in part]
         return pltpu.roll(part[0], 1, 1) + part[1] + pltpu.roll(part[2], pitch - 1, 1)
 
-    size1 = fits(C + 2, pitch, 320)
-    size2 = fits(C, pitch, 400)
+    size1 = fits(C + 2, pitch, 480)
+    size2 = fits(C, pitch, 640)
 
     def stem(b):
         for i, (dg, ds) in enumerate(DIRS):

time: 91.4 us -> 87.2 us (0.954)
  Pallas kernels: 88.1 us -> 84 us
    pallas_call x1, Pallas kernels: 88.1 us -> 84 us  [shards(): pl.pallas_call(functools.partial(kernel, (S, N, B, R, C, K1, K2)), out_sh...]
where the time goes in v5:
time: 87.2 us; the launch traced here: 87.1 us
  Pallas kernels  84 us (96%)
  local copies, waits for them, and re-layouts  3.13 us (4%)
    pallas_call x1, Pallas kernels, shards(): pl.pallas_call(functools.partial(kernel, (S, N, B, R, C, K1, K2)), out_sh...  84 us
    unnamed x1, local copies, waits for them, and re-layouts  3.13 us

profile of v5, /device:TPU:11, one launch (start us, length us, event | category | flops | bytes accessed | tf_op | source)
XLA Modules:
  0.0 87.1 jit_solution(12666568740034235437)
XLA Ops:
  0.0 84.0 %shard_map.55 = bf16[1,2,16,64,512]{4,3,2,1,0:T(8,128)(2,1)} custom-call(bf16[2,64,16,256]{3,2,1,0:T(8,128)(2,1)} %feat.1, bf16[3,3,256,256]{3,2,1,0:T(8,128)(2,1)} %wf.1, bf16[3,3,256,256]{3,2,1,0:T(8,128)(2,1)} %ws.1, bf16[2,2,256,512]{3,2,1,0:T(8,128)(2,1)} %wd.1, bf16[1,3,3,512,512]{4,3,2,1,0:T(8,128)(2,1)} %wsec.1), custom_call_target="tpu_custom_call" | custom-call | flops 15032385536 | bytes 16777216 | tf_op jit(solution)/shard_map/pallas_call | solution.py:521
  84.0 3.1 %copy.7 = bf16[1,2,16,64,512]{4,3,2,1,0:T(8,128)(2,1)} copy(bf16[1,2,16,64,512]{4,3,2,1,0:T(8,128)(2,1)} %shard_map.55) | data formatting | bytes 4194304

commit v6 on v5

--- a/solution.py
+++ b/solution.py
@@ -379,7 +379,7 @@
         )
 
     span = cr * cols
-    width = 256
+    width = K2
 
     def order(p):
         return jnp.where(p == n - 1, n - 1, jnp.where(p == n - 2, 0, p + 1))

time: 87.2 us -> 87.3 us (level)
  no operation moved by 1% of the time
where the time goes in v6:
time: 87.3 us; the launch traced here: 87.2 us
  Pallas kernels  84.1 us (96%)
  local copies, waits for them, and re-layouts  3.13 us (4%)
    pallas_call x1, Pallas kernels, shards(): pl.pallas_call(functools.partial(kernel, (S, N, B, R, C, K1, K2)), out_sh...  84.1 us
    unnamed x1, local copies, waits for them, and re-layouts  3.13 us

profile of v6, /device:TPU:11, one launch (start us, length us, event | category | flops | bytes accessed | tf_op | source)
XLA Modules:
  0.0 87.2 jit_solution(2540030210847073089)
XLA Ops:
  0.0 84.1 %shard_map.55 = bf16[1,2,16,64,512]{4,3,2,1,0:T(8,128)(2,1)} custom-call(bf16[2,64,16,256]{3,2,1,0:T(8,128)(2,1)} %feat.1, bf16[3,3,256,256]{3,2,1,0:T(8,128)(2,1)} %wf.1, bf16[3,3,256,256]{3,2,1,0:T(8,128)(2,1)} %ws.1, bf16[2,2,256,512]{3,2,1,0:T(8,128)(2,1)} %wd.1, bf16[1,3,3,512,512]{4,3,2,1,0:T(8,128)(2,1)} %wsec.1), custom_call_target="tpu_custom_call" | custom-call | flops 15032385536 | bytes 16777216 | tf_op jit(solution)/shard_map/pallas_call | solution.py:521
  84.1 3.1 %copy.7 = bf16[1,2,16,64,512]{4,3,2,1,0:T(8,128)(2,1)} copy(bf16[1,2,16,64,512]{4,3,2,1,0:T(8,128)(2,1)} %shard_map.55) | data formatting | bytes 4194304
